TPU v7x, 512 devices: a whole 4x4x16 slice. The times are simulated.
512 devices in a mesh: ctx: 64 (over y, z), uly: 8 (over x, core).
Axes of the slice: x: 4, y: 4, z: 16, core: 2. Of those that a mesh axis runs over, the one named last changes fastest.
Arguments:
- lin_query: bfloat16 [32768, 4096], P(('ctx', 'uly')), may hold values from -5 to 5
- lin_key: bfloat16 [32768, 4096], P(('ctx', 'uly')), may hold values from -5 to 5
- lin_value: bfloat16 [32768, 4096], P(('ctx', 'uly')), may hold values from -60 to 60
- log_decay: bfloat16 [32768, 32], P(('ctx', 'uly')), may hold values from 0 to 1
- norm_gain: float32 [4096], P('uly'), may hold values from 0.25 to 1.75
- doc_lengths: int32 [64], replicated, may hold values from 1 to 1024, 32768 in all
- att_query: bfloat16 [32768, 4096], P(('ctx', 'uly')), may hold values from -6 to 6
- att_key: bfloat16 [32768, 1024], P(('ctx', 'uly')), may hold values from -6 to 6
- att_value: bfloat16 [32768, 1024], P(('ctx', 'uly')), may hold values from -5 to 5
Outputs:
- lin_out: bfloat16 [32768, 4096], P('ctx', 'uly')
- att_out: bfloat16 [32768, 4096], P('ctx', 'uly')
Inputs may be any that keep to these rules, and one draw needn't show every extreme that they name: `doc_lengths`: documents follow one another from position 0 and fill the sequence; the longest has exactly 1024 positions.
All inputs are finite; a program needn't handle non-finite values.
Results may differ from a plain program's by a relative error of at most 0.008.
Values may be sent and summed in bfloat16 or wider, within the bound.
No kernel may reach another device: no remote copies, remote signals or barrier semaphores. Data moves between devices by JAX's collectives and lax.ppermute only.
A program may use at most 128 MiB of HBM per device.

v0:
```python
import jax
import jax.numpy as jnp
from jax import lax
from jax.sharding import PartitionSpec as P

HEAD = 128
WIN = 2


def prefix(x, axis, join, neutral):
    place = lax.axis_index(axis)
    gathered = jax.tree.map(
        lambda a, kind: lax.all_gather(a.astype(kind), axis), x, (jnp.bfloat16, jnp.bfloat16)
    )
    state = jax.tree.map(lambda a, e: jnp.zeros_like(a) + jnp.asarray(e, a.dtype), x, neutral)

    def one(turn, state):
        return join(
            state,
            jax.tree.map(
                lambda a, own: lax.dynamic_index_in_dim(a, turn, 0, False).astype(own.dtype),
                gathered,
                x,
            ),
        )

    return lax.fori_loop(0, place, one, state)


def shifted(block, axis, distance):
    devices = range(lax.axis_size(axis))
    route = [(i - distance, i) for i in devices if i - distance in devices]
    return lax.ppermute(block, axis, route)


def doc_begin(positions, doc_lengths):
    start_pos = jnp.cumsum(doc_lengths) - doc_lengths
    covered = start_pos[None, :] <= positions[:, None]
    return jnp.max(jnp.where(covered, start_pos[None, :], 0), axis=1)


def combine_states(earlier, later_part):
    return (earlier[0] * later_part[0], later_part[0][:, None, None] * earlier[1] + later_part[1])


def shards(
    lin_query, lin_key, lin_value, log_decay, norm_gain, doc_lengths, att_query, att_key, att_value
):
    query_in, key_in, value_in, decay_in, att_q, att_k, att_v = (
        lax.all_to_all(lin_query, "uly", split_axis=1, concat_axis=0, tiled=True),
        lax.all_to_all(lin_key, "uly", split_axis=1, concat_axis=0, tiled=True),
        lax.all_to_all(lin_value, "uly", split_axis=1, concat_axis=0, tiled=True),
        lax.all_to_all(log_decay, "uly", split_axis=1, concat_axis=0, tiled=True),
        lax.all_to_all(att_query, "uly", split_axis=1, concat_axis=0, tiled=True),
        lax.all_to_all(att_key, "uly", split_axis=1, concat_axis=0, tiled=True),
        lax.all_to_all(att_value, "uly", split_axis=1, concat_axis=0, tiled=True),
    )
    block_len = query_in.shape[0]
    head_count = decay_in.shape[1]
    block_start = lax.axis_index("ctx") * block_len
    offsets = jnp.arange(block_len, dtype=jnp.int32)
    positions = block_start + offsets
    token_begin = doc_begin(positions, doc_lengths)
    decay_sum = jnp.cumsum(decay_in.astype(jnp.float32), axis=0)
    query_map = jax.nn.silu(
        query_in.reshape(block_len, head_count, HEAD).astype(jnp.float32)
    ).astype(jnp.bfloat16)
    key_map = jax.nn.silu(key_in.reshape(block_len, head_count, HEAD).astype(jnp.float32)).astype(
        jnp.bfloat16
    )
    values = value_in.reshape(block_len, head_count, HEAD)
    scores = jnp.einsum("thd,shd->hts", query_map, key_map, preferred_element_type=jnp.float32)
    same_doc = (offsets[None, :] <= offsets[:, None]) & (
        token_begin[None, :] == token_begin[:, None]
    )
    decay_gap = decay_sum.T[:, :, None] - decay_sum.T[:, None, :]
    weights = jnp.where(same_doc[None], jnp.exp(-jnp.where(same_doc[None], decay_gap, 0.0)), 0.0)
    weighted_scores = (weights * scores).astype(jnp.bfloat16)
    inside = jnp.einsum("hts,shd->thd", weighted_scores, values, preferred_element_type=jnp.float32)
    last_begin = token_begin[block_len - 1]
    end_weight = jnp.where(
        (token_begin == last_begin)[:, None],
        jnp.exp(decay_sum - decay_sum[block_len - 1][None, :]),
        0.0,
    )
    end_keys = (key_map.astype(jnp.float32) * end_weight[:, :, None]).astype(jnp.bfloat16)
    end_state = jnp.einsum("shd,she->hde", end_keys, values, preferred_element_type=jnp.float32)
    block_decay = jnp.where(last_begin < block_start, jnp.exp(-decay_sum[block_len - 1]), 0.0)
    identity = (jnp.ones_like(block_decay), jnp.zeros_like(end_state))
    _, incoming = prefix((block_decay, end_state), "ctx", combine_states, identity)
    entry_decay = jnp.where((token_begin < block_start)[:, None], jnp.exp(-decay_sum), 0.0)
    carried = (
        jnp.einsum(
            "thd,hde->the",
            query_map,
            incoming.astype(jnp.bfloat16),
            preferred_element_type=jnp.float32,
        )
        * entry_decay[:, :, None]
    )
    combined = inside + carried
    normed = (
        combined
        * lax.rsqrt(jnp.mean(combined * combined, axis=-1, keepdims=True) + 1e-06)
        * norm_gain.reshape(head_count, HEAD)
    )
    lin_out = normed.astype(jnp.bfloat16).reshape(block_len, head_count * HEAD)
    kv_heads = att_k.shape[1] // HEAD
    group_size = att_q.shape[1] // (kv_heads * HEAD)
    queries = att_q.reshape(block_len, kv_heads, group_size, HEAD)
    score_scale = HEAD ** (-0.5)

    def attend(state_carry, key_block, value_block, key_position):
        row_max, row_total, accumulated = state_carry
        key_begin = doc_begin(key_position, doc_lengths)
        allowed = (
            (key_position[None, :] <= positions[:, None])
            & (key_position[None, :] >= 0)
            & (key_begin[None, :] == token_begin[:, None])
        )
        block_scores = (
            jnp.einsum(
                "tkgd,skd->kgts",
                queries,
                key_block.reshape(block_len, kv_heads, HEAD),
                preferred_element_type=jnp.float32,
            )
            * score_scale
        )
        new_max = jnp.maximum(row_max, jnp.max(jnp.where(allowed, block_scores, -1e30), axis=-1))
        att_weights = jnp.where(allowed, jnp.exp(block_scores - new_max[..., None]), 0.0)
        shrink = jnp.exp(row_max - new_max)
        row_total = row_total * shrink + jnp.sum(att_weights, axis=-1)
        products = jnp.einsum(
            "kgts,skd->tkgd",
            att_weights.astype(jnp.bfloat16),
            value_block.reshape(block_len, kv_heads, HEAD),
            preferred_element_type=jnp.float32,
        )
        accumulated = accumulated * jnp.transpose(shrink, (2, 0, 1))[..., None] + products
        return (new_max, row_total, accumulated)

    state_carry = (
        jnp.full((kv_heads, group_size, block_len), -1e30, jnp.float32),
        jnp.zeros((kv_heads, group_size, block_len), jnp.float32),
        jnp.zeros((block_len, kv_heads, group_size, HEAD), jnp.float32),
    )
    state_carry = attend(state_carry, att_k, att_v, positions)
    for distance in range(1, WIN + 1):
        earlier_keys, earlier_values = shifted((att_k, att_v), "ctx", distance)
        key_position = positions - distance * block_len
        state_carry = attend(state_carry, earlier_keys, earlier_values, key_position)
    row_max, row_total, accumulated = state_carry
    att_out = (
        (accumulated / jnp.transpose(row_total, (2, 0, 1))[..., None])
        .astype(jnp.bfloat16)
        .reshape(block_len, kv_heads * group_size * HEAD)
    )
    return (lin_out, att_out)


def solution(mesh):
    placed = (
        P(("ctx", "uly"), None),
        P(("ctx", "uly"), None),
        P(("ctx", "uly"), None),
        P(("ctx", "uly"), None),
        P("uly"),
        P(),
        P(("ctx", "uly"), None),
        P(("ctx", "uly"), None),
        P(("ctx", "uly"), None),
    )
    return jax.shard_map(
        shards,
        mesh=mesh,
        in_specs=placed,
        out_specs=(P("ctx", "uly"), P("ctx", "uly")),
        check_vma=False,
    )
```

profile of v0, /device:TPU:510, one launch (start us, length us, event | category | flops | bytes accessed | tf_op | source)
XLA Modules:
  0.0 326.6 jit_solution(10978063020451155656)
XLA Ops:
  7.2 1.4 reshape.440
  8.6 4.8 %all-to-all-start = ((bf16[8,2,128]{2,1,0:T(2,128)(2,1)}), bf16[8,2,128]{2,1,0:T(2,128)(2,1)S(1)}, u32[]{:S(2)}, u32[]{:S(2)}) async-start(bf16[8,2,128]{2,1,0:T(2,128)(2,1)} %reshape.440), calls=%async_computation | async-start | bytes 8192 | tf_op jit(solution)/shard_map/all_to_all | solution.py:53
  17.6 1.9 copy.240
  19.5 1.9 copy.239
  21.4 4.8 %all-to-all-start.2 = ((bf16[64,8,512]{2,0,1:T(8,128)(2,1)}), bf16[64,8,512]{2,0,1:T(8,128)(2,1)S(1)}, u32[]{:S(2)}, u32[]{:S(2)}) async-start(bf16[64,8,512]{2,0,1:T(8,128)(2,1)} %bitcast.306), calls=%async_computation.2 | async-start | bytes 1048576 | tf_op jit(solution)/shard_map/all_to_all | solution.py:51
  26.4 1.2 reduce-window.20
  28.8 5.7 %all-to-all-done.2 = bf16[64,8,512]{2,0,1:T(8,128)(2,1)S(1)} async-done(((bf16[64,8,512]{2,0,1:T(8,128)(2,1)}), bf16[64,8,512]{2,0,1:T(8,128)(2,1)S(1)}, u32[]{:S(2)}, u32[]{:S(2)}) %all-to-all-start.2) | async-done | bytes 524320 | tf_op jit(solution)/shard_map/all_to_all | solution.py:51
  34.5 5.5 %all-to-all-start.3 = ((bf16[64,8,512]{2,0,1:T(8,128)(2,1)}), bf16[64,8,512]{2,0,1:T(8,128)(2,1)S(1)}, u32[]{:S(2)}, u32[]{:S(2)}) async-start(bf16[64,8,512]{2,0,1:T(8,128)(2,1)} %bitcast.305), calls=%async_computation.3 | async-start | bytes 1048576 | tf_op jit(solution)/shard_map/all_to_all | solution.py:52
  41.6 6.7 %all-to-all-done.3 = bf16[64,8,512]{2,0,1:T(8,128)(2,1)S(1)} async-done(((bf16[64,8,512]{2,0,1:T(8,128)(2,1)}), bf16[64,8,512]{2,0,1:T(8,128)(2,1)S(1)}, u32[]{:S(2)}, u32[]{:S(2)}) %all-to-all-start.3) | async-done | bytes 524320 | tf_op jit(solution)/shard_map/all_to_all | solution.py:52
  48.4 1.5 convolution_convert_fusion
  50.6 6.0 %all-to-all-start.4 = ((bf16[64,8,128]{2,0,1:T(8,128)(2,1)}), bf16[64,8,128]{2,0,1:T(8,128)(2,1)}, u32[]{:S(2)}, u32[]{:S(2)}) async-start(bf16[64,8,128]{2,0,1:T(8,128)(2,1)} %copy_bitcast_fusion.5), calls=%async_computation.4 | async-start | bytes 262144 | tf_op jit(solution)/shard_map/all_to_all | solution.py:55
  57.3 3.5 %all-to-all-done.4 = bf16[64,8,128]{2,0,1:T(8,128)(2,1)} async-done(((bf16[64,8,128]{2,0,1:T(8,128)(2,1)}), bf16[64,8,128]{2,0,1:T(8,128)(2,1)}, u32[]{:S(2)}, u32[]{:S(2)}) %all-to-all-start.4) | async-done | bytes 131104 | tf_op jit(solution)/shard_map/all_to_all | solution.py:55
  60.7 5.4 %all-to-all-start.6 = ((bf16[64,8,128]{2,0,1:T(8,128)(2,1)}), bf16[64,8,128]{2,0,1:T(8,128)(2,1)S(1)}, u32[]{:S(2)}, u32[]{:S(2)}) async-start(bf16[64,8,128]{2,0,1:T(8,128)(2,1)} %copy_bitcast_fusion.4), calls=%async_computation.6 | async-start | bytes 262144 | tf_op jit(solution)/shard_map/all_to_all | solution.py:56
  67.0 3.2 all-to-all-done.6
  70.2 5.5 %all-to-all-start.5 = ((bf16[64,8,512]{2,0,1:T(8,128)(2,1)}), bf16[64,8,512]{2,0,1:T(8,128)(2,1)S(1)}, u32[]{:S(2)}, u32[]{:S(2)}) async-start(bf16[64,8,512]{2,0,1:T(8,128)(2,1)} %bitcast.304), calls=%async_computation.5 | async-start | bytes 1048576 | tf_op jit(solution)/shard_map/all_to_all | solution.py:54
  75.7 2.4 compare_and_fusion
  80.2 70.8 %all-gather.1 = bf16[64,1,4]{2,1,0:T(2,128)(2,1)S(1)} all-gather(bf16[1,1,4]{2,1,0:T(2,128)(2,1)} %get-tuple-element.102), channel_id=1, replica_groups=mesh['ctx'=64,'uly'=8] {'ctx'}, dimensions={0}, use_global_device_ids=true | all-gather | bytes 520 | tf_op jit(solution)/shard_map/all_gather | solution.py:13
  152.0 1.3 collective-permute-start.2
  153.3 1.3 collective-permute-start
  154.6 1.7 copy.181
  156.3 1.3 collective-permute-start.3
  157.6 1.3 collective-permute-start.1
  158.9 4.8 %all-to-all-start.1 = ((bf16[64,8,512]{2,0,1:T(8,128)(2,1)}), bf16[64,8,512]{2,0,1:T(8,128)(2,1)S(1)}, u32[]{:S(2)}, u32[]{:S(2)}) async-start(bf16[64,8,512]{2,0,1:T(8,128)(2,1)} %bitcast.307), calls=%async_computation.1 | async-start | bytes 1048576 | tf_op jit(solution)/shard_map/all_to_all | solution.py:50
  163.8 1.8 fusion.6
  165.6 1.8 fusion
  167.4 1.8 fusion.3
  173.1 3.3 collective-permute-done.3
  176.3 2.0 fusion.29
  178.4 2.1 divide_convert_fusion
  182.0 3.5 %fusion.28 = f32[512,4,128]{0,2,1:T(8,128)S(1)} fusion(f32[4,512]{1,0:T(4,128)S(1)} %bitcast.327, pred[512,512]{1,0:T(8,128)(4,1)} %get-tuple-element.111, bf16[512,4,128]{2,1,0:T(4,128)(2,1)} %copy-done.4, f32[512,4,128]{2,1,0:T(4,128)S(1)} %reshape.426, f32[512,4,128]{2,1,0:T(4,128)S(1)} %reshape.427), kind=kOutput, calls=%fused_computation.34 | convolution fusion | flops 545783808 | bytes 3940352 | tf_op jit(solution)/shard_map/hts,shd->thd/dot_general | solution.py:79
  185.4 25.0 %all-gather.4.cloned.1.call-done = bf16[256,128,128]{2,1,0:T(8,128)(2,1)} async-done(((bf16[4,128,128]{2,1,0:T(8,128)(2,1)}), bf16[256,128,128]{2,1,0:T(8,128)(2,1)}) %all-gather.4.cloned.1.call-update) | async-done | bytes 8388624 | tf_op jit(solution)/shard_map/all_gather | solution.py:13
  210.4 107.6 %while.12 = (s32[]{:T(128)}, f32[4,128,128]{2,1,0:T(8,128)S(1)}, s32[]{:T(128)}, bf16[64,4]{1,0:T(8,128)(2,1)}, bf16[64,4,128,128]{3,2,1,0:T(8,128)(2,1)}, /*index=5*/s32[]{:T(128)}, s32[]{:T(128)}, s32[]{:T(128)}) while((s32[]{:T(128)}, f32[4,128,128]{2,1,0:T(8,128)S(1)}, s32[]{:T(128)}, bf16[64,4]{1,0:T(8,128)(2,1)}, ...), condition=%wide.region_5.6_spmd, body=%wide.region_4.5_spmd.sunk | while | flops 196617 | bytes 655527 | solution.py:27
  211.2 1.0 convert_add_fusion.2
  212.9 1.0 convert_add_fusion.2
  214.6 1.0 convert_add_fusion.2
  216.3 1.0 convert_add_fusion.2
  218.1 1.0 convert_add_fusion.2
  219.8 1.0 convert_add_fusion.2
  221.5 1.0 convert_add_fusion.2
  223.3 1.0 convert_add_fusion.2
  225.0 1.0 convert_add_fusion.2
  226.7 1.0 convert_add_fusion.2
  228.4 1.0 convert_add_fusion.2
  230.1 1.0 convert_add_fusion.2
  231.9 1.0 convert_add_fusion.2
  233.6 1.0 convert_add_fusion.2
  235.3 1.0 convert_add_fusion.2
  237.0 1.0 convert_add_fusion.2
  (192 shorter events, 108.6 us)
Async XLA Ops:
  7.2 42.7 %copy-start = (bf16[64,1024]{1,0:T(8,128)(2,1)S(1)}, bf16[64,1024]{1,0:T(8,128)(2,1)}, u32[]{:S(2)}) copy-start(bf16[64,1024]{1,0:T(8,128)(2,1)} %param.18) | copy-start | bytes 393220
  8.6 12.8 %all-to-all-start = ((bf16[8,2,128]{2,1,0:T(2,128)(2,1)}), bf16[8,2,128]{2,1,0:T(2,128)(2,1)S(1)}, u32[]{:S(2)}, u32[]{:S(2)}) async-start(bf16[8,2,128]{2,1,0:T(2,128)(2,1)} %reshape.440), calls=%async_computation | async-start | bytes 8192 | tf_op jit(solution)/shard_map/all_to_all | solution.py:53
  13.4 8.0 %copy-start.9 = (s32[512]{0:T(512)}, s32[512]{0:T(512)S(1)}, u32[]{:S(2)}) copy-start(s32[512]{0:T(512)S(1)} %get-tuple-element.123) | copy-start | bytes 6148
  13.4 8.0 %copy-start.8 = (s32[512]{0:T(512)}, s32[512]{0:T(512)S(1)}, u32[]{:S(2)}) copy-start(s32[512]{0:T(512)S(1)} %fusion.81) | copy-start | bytes 6148
  21.4 13.1 %all-to-all-start.2 = ((bf16[64,8,512]{2,0,1:T(8,128)(2,1)}), bf16[64,8,512]{2,0,1:T(8,128)(2,1)S(1)}, u32[]{:S(2)}, u32[]{:S(2)}) async-start(bf16[64,8,512]{2,0,1:T(8,128)(2,1)} %bitcast.306), calls=%async_computation.2 | async-start | bytes 1048576 | tf_op jit(solution)/shard_map/all_to_all | solution.py:51
  34.5 13.8 %all-to-all-start.3 = ((bf16[64,8,512]{2,0,1:T(8,128)(2,1)}), bf16[64,8,512]{2,0,1:T(8,128)(2,1)S(1)}, u32[]{:S(2)}, u32[]{:S(2)}) async-start(bf16[64,8,512]{2,0,1:T(8,128)(2,1)} %bitcast.305), calls=%async_computation.3 | async-start | bytes 1048576 | tf_op jit(solution)/shard_map/all_to_all | solution.py:52
  40.0 170.4 %all-gather.4.cloned.1.call-start = ((), (), s32[]{:S(2)}) async-start(), calls=%async_computation.7 | async-start | bytes 8519680 | tf_op jit(solution)/shard_map/all_gather | solution.py:13
  41.5 15.1 %copy-start.7 = (bf16[64,1024]{1,0:T(8,128)(2,1)S(1)}, bf16[64,1024]{1,0:T(8,128)(2,1)}, u32[]{:S(2)}) copy-start(bf16[64,1024]{1,0:T(8,128)(2,1)} %param.19) | copy-start | bytes 393220
  41.5 24.6 %copy-start.2 = (bf16[64,4096]{1,0:T(8,128)(2,1)S(1)}, bf16[64,4096]{1,0:T(8,128)(2,1)}, u32[]{:S(2)}) copy-start(bf16[64,4096]{1,0:T(8,128)(2,1)} %param.17) | copy-start | bytes 1572868
  48.4 21.8 %copy-start.4 = (bf16[512,4,128]{2,1,0:T(4,128)(2,1)}, bf16[512,4,128]{2,1,0:T(4,128)(2,1)S(1)}, u32[]{:S(2)}) copy-start(bf16[512,4,128]{2,1,0:T(4,128)(2,1)S(1)} %reshape.414) | copy-start | bytes 1572868
  49.9 29.5 %copy-start.3 = (bf16[64,4096]{1,0:T(8,128)(2,1)S(1)}, bf16[64,4096]{1,0:T(8,128)(2,1)}, u32[]{:S(2)}) copy-start(bf16[64,4096]{1,0:T(8,128)(2,1)} %param.11) | copy-start | bytes 1572868
  49.9 102.0 %copy-start.1 = (f32[512,4]{1,0:T(8,128)S(1)}, f32[512,4]{1,0:T(8,128)}, u32[]{:S(2)}) copy-start(f32[512,4]{1,0:T(8,128)} %get-tuple-element.100) | copy-start | bytes 24580
  50.6 10.1 %all-to-all-start.4 = ((bf16[64,8,128]{2,0,1:T(8,128)(2,1)}), bf16[64,8,128]{2,0,1:T(8,128)(2,1)}, u32[]{:S(2)}, u32[]{:S(2)}) async-start(bf16[64,8,128]{2,0,1:T(8,128)(2,1)} %copy_bitcast_fusion.5), calls=%async_computation.4 | async-start | bytes 262144 | tf_op jit(solution)/shard_map/all_to_all | solution.py:55
  60.7 9.4 %all-to-all-start.6 = ((bf16[64,8,128]{2,0,1:T(8,128)(2,1)}), bf16[64,8,128]{2,0,1:T(8,128)(2,1)S(1)}, u32[]{:S(2)}, u32[]{:S(2)}) async-start(bf16[64,8,128]{2,0,1:T(8,128)(2,1)} %copy_bitcast_fusion.4), calls=%async_computation.6 | async-start | bytes 262144 | tf_op jit(solution)/shard_map/all_to_all | solution.py:56
  70.2 5.5 %copy-start.5 = (bf16[64,8,128]{2,0,1:T(8,128)(2,1)}, bf16[64,8,128]{2,0,1:T(8,128)(2,1)S(1)}, u32[]{:S(2)}) copy-start(bf16[64,8,128]{2,0,1:T(8,128)(2,1)S(1)} %all-to-all-done.6) | copy-start | bytes 393220
  70.2 88.7 %all-to-all-start.5 = ((bf16[64,8,512]{2,0,1:T(8,128)(2,1)}), bf16[64,8,512]{2,0,1:T(8,128)(2,1)S(1)}, u32[]{:S(2)}, u32[]{:S(2)}) async-start(bf16[64,8,512]{2,0,1:T(8,128)(2,1)} %bitcast.304), calls=%async_computation.5 | async-start | bytes 1048576 | tf_op jit(solution)/shard_map/all_to_all | solution.py:54
  152.0 13.6 %collective-permute-start.2 = (bf16[512,128]{1,0:T(8,128)(2,1)}, bf16[512,128]{1,0:T(8,128)(2,1)}, u32[]{:S(2)}, u32[]{:S(2)}) collective-permute-start(bf16[512,128]{1,0:T(8,128)(2,1)} %bitcast.20), channel_id=1, source_target_pairs={{0,16},{8,24},{16,32},{24,40},{32,48},{40,56},{48,64},{56,72},{64,... | collective-permute-start | bytes 393224 | tf_op jit(solution)/shard_map/ppermute | solution.py:33
  153.3 14.1 %collective-permute-start = (bf16[512,128]{1,0:T(8,128)(2,1)}, bf16[512,128]{1,0:T(8,128)(2,1)}, u32[]{:S(2)}, u32[]{:S(2)}) collective-permute-start(bf16[512,128]{1,0:T(8,128)(2,1)} %bitcast.20), channel_id=1, source_target_pairs={{0,8},{8,16},{16,24},{24,32},{32,40},{40,48},{48,56},{56,64},{64,7... | collective-permute-start | bytes 393224 | tf_op jit(solution)/shard_map/ppermute | solution.py:33
  156.3 20.1 %collective-permute-start.3 = (bf16[512,128]{0,1:T(8,128)(2,1)}, bf16[512,128]{0,1:T(8,128)(2,1)}, u32[]{:S(2)}, u32[]{:S(2)}) collective-permute-start(bf16[512,128]{0,1:T(8,128)(2,1)} %copy.181), channel_id=1, source_target_pairs={{0,16},{8,24},{16,32},{24,40},{32,48},{40,56},{48,64},{56,72},{64,... | collective-permute-start | bytes 393224 | tf_op jit(solution)/shard_map/ppermute | solution.py:33
  157.6 20.8 %collective-permute-start.1 = (bf16[512,128]{0,1:T(8,128)(2,1)}, bf16[512,128]{0,1:T(8,128)(2,1)}, u32[]{:S(2)}, u32[]{:S(2)}) collective-permute-start(bf16[512,128]{0,1:T(8,128)(2,1)} %copy.181), channel_id=1, source_target_pairs={{0,8},{8,16},{16,24},{24,32},{32,40},{40,48},{48,56},{56,64},{64,7... | collective-permute-start | bytes 393224 | tf_op jit(solution)/shard_map/ppermute | solution.py:33
  158.9 22.6 %all-to-all-start.1 = ((bf16[64,8,512]{2,0,1:T(8,128)(2,1)}), bf16[64,8,512]{2,0,1:T(8,128)(2,1)S(1)}, u32[]{:S(2)}, u32[]{:S(2)}) async-start(bf16[64,8,512]{2,0,1:T(8,128)(2,1)} %bitcast.307), calls=%async_computation.1 | async-start | bytes 1048576 | tf_op jit(solution)/shard_map/all_to_all | solution.py:50
  170.2 1.9 copy-start.6
  210.4 108.2 %copy-start.10 = (f32[512]{0:T(512)S(1)}, f32[512]{0:T(512)}, u32[]{:S(2)}) copy-start(f32[512]{0:T(512)} %param.15) | copy-start | bytes 6148
Sparse Core Ops, SparseCore 0:
  50.0 160.3 all-gather.3
where the time goes:
time: 330 us; the launch traced here: 327 us
  other arithmetic  117 us (35%)
  blocking collectives  70.8 us (21%)
  waiting for transfers between devices  47.3 us (14%)
  starting transfers between devices  41.9 us (13%)
  local copies, waits for them, and re-layouts  17 us (5%)
  matrix products  16 us (5%)
  between operations  15 us (5%)
    all_gather x1, blocking collectives, prefix(): lax.all_gather(a.astype(kind), axis)  70.8 us
    add x63, other arithmetic, combine_states(): later_part[0][:, None, None] * earlier[1] + later_part[1]  63.7 us
    convert_element_type x63, other arithmetic, one(): lax.dynamic_index_in_dim(a, turn, 0, False).astype(own.dtype)  42.1 us
    all_gather x1, waiting for transfers between devices, prefix(): lax.all_gather(a.astype(kind), axis)  25 us
    all_to_all x1, waiting for transfers between devices, shards(): lax.all_to_all(lin_value, 'uly', split_axis=1, concat_axis=0, tiled=True)  6.71 us
  transfers between devices with their start and end apart: 12, of which 6 were waited for; matrix products, arithmetic and copies ran while one was open for 12% of the time, Pallas kernels for 0%

commit v1 on v0

--- a/solution.py
+++ b/solution.py
@@ -5,6 +5,18 @@
 
 HEAD = 128
 WIN = 2
+
+
+def exchange_directly(value, axis, split, join):
+    ways, here = (lax.axis_size(axis), lax.axis_index(axis))
+    width = value.shape[split] // ways
+    turned = jnp.roll(value, -here * width, axis=split)
+    got = [lax.slice_in_dim(turned, 0, width, axis=split)]
+    for far in range(1, ways):
+        sent = lax.slice_in_dim(turned, far * width, (far + 1) * width, axis=split)
+        got.append(lax.ppermute(sent, axis, [(d, (d + far) % ways) for d in range(ways)]))
+    line = jnp.concatenate(got[::-1], axis=join)
+    return jnp.roll(line, (here + 1) * got[0].shape[join], axis=join)
 
 
 def prefix(x, axis, join, neutral):
@@ -53,7 +65,7 @@
         lax.all_to_all(log_decay, "uly", split_axis=1, concat_axis=0, tiled=True),
         lax.all_to_all(att_query, "uly", split_axis=1, concat_axis=0, tiled=True),
         lax.all_to_all(att_key, "uly", split_axis=1, concat_axis=0, tiled=True),
-        lax.all_to_all(att_value, "uly", split_axis=1, concat_axis=0, tiled=True),
+        exchange_directly(att_value, "uly", 1, 0),
     )
     block_len = query_in.shape[0]
     head_count = decay_in.shape[1]

time: 330 us -> 336 us (1.018)
  the two profiles are of different devices: /device:TPU:510 before, /device:TPU:506 now
where the time goes in v1:
time: 336 us; the launch traced here: 332 us
  other arithmetic  117 us (35%)
  blocking collectives  70.3 us (21%)
  starting transfers between devices  51.8 us (15%)
  waiting for transfers between devices  37.6 us (11%)
  matrix products  19.2 us (6%)
  local copies, waits for them, and re-layouts  18.5 us (6%)
  between operations  15.2 us (5%)
    all_gather x1, blocking collectives, prefix(): lax.all_gather(a.astype(kind), axis)  70.3 us
    add x63, other arithmetic, combine_states(): later_part[0][:, None, None] * earlier[1] + later_part[1]  63.7 us
    convert_element_type x63, other arithmetic, one(): lax.dynamic_index_in_dim(a, turn, 0, False).astype(own.dtype)  42.5 us
    ppermute x7, starting transfers between devices, exchange_directly(): lax.ppermute(sent, axis, [(d, (d + far) % ways) for d in range(ways)])  16.3 us
    ppermute x4, waiting for transfers between devices, shifted(): return lax.ppermute(block, axis, route)  13 us
    all_gather x1, waiting for transfers between devices, prefix(): lax.all_gather(a.astype(kind), axis)  10.8 us
    all_to_all x1, waiting for transfers between devices, shards(): lax.all_to_all(lin_value, 'uly', split_axis=1, concat_axis=0, tiled=True)  7.39 us
  transfers between devices with their start and end apart: 18, of which 4 were waited for; matrix products, arithmetic and copies ran while one was open for 13% of the time, Pallas kernels for 0%

profile of v1, /device:TPU:506, one launch (start us, length us, event | category | flops | bytes accessed | tf_op | source)
XLA Modules:
  0.0 331.7 jit_solution(14348528047238575889)
XLA Ops:
  7.2 1.4 reshape.433
  8.6 4.8 %all-to-all-start = ((bf16[8,2,128]{2,1,0:T(2,128)(2,1)}), bf16[8,2,128]{2,1,0:T(2,128)(2,1)S(1)}, u32[]{:S(2)}, u32[]{:S(2)}) async-start(bf16[8,2,128]{2,1,0:T(2,128)(2,1)} %reshape.433), calls=%async_computation | async-start | bytes 8192 | tf_op jit(solution)/shard_map/all_to_all | solution.py:65
  17.7 1.9 copy.197
  19.6 1.9 copy.196
  21.5 4.8 %all-to-all-start.2 = ((bf16[64,8,512]{2,0,1:T(8,128)(2,1)}), bf16[64,8,512]{2,0,1:T(8,128)(2,1)S(1)}, u32[]{:S(2)}, u32[]{:S(2)}) async-start(bf16[64,8,512]{2,0,1:T(8,128)(2,1)} %bitcast.292), calls=%async_computation.2 | async-start | bytes 1048576 | tf_op jit(solution)/shard_map/all_to_all | solution.py:63
  26.5 1.2 reduce-window.20
  28.8 6.3 %all-to-all-done.2 = bf16[64,8,512]{2,0,1:T(8,128)(2,1)S(1)} async-done(((bf16[64,8,512]{2,0,1:T(8,128)(2,1)}), bf16[64,8,512]{2,0,1:T(8,128)(2,1)S(1)}, u32[]{:S(2)}, u32[]{:S(2)}) %all-to-all-start.2) | async-done | bytes 524320 | tf_op jit(solution)/shard_map/all_to_all | solution.py:63
  35.1 4.9 %all-to-all-start.3 = ((bf16[64,8,512]{2,0,1:T(8,128)(2,1)}), bf16[64,8,512]{2,0,1:T(8,128)(2,1)S(1)}, u32[]{:S(2)}, u32[]{:S(2)}) async-start(bf16[64,8,512]{2,0,1:T(8,128)(2,1)} %bitcast.291), calls=%async_computation.3 | async-start | bytes 1048576 | tf_op jit(solution)/shard_map/all_to_all | solution.py:64
  41.5 7.4 %all-to-all-done.3 = bf16[64,8,512]{2,0,1:T(8,128)(2,1)S(1)} async-done(((bf16[64,8,512]{2,0,1:T(8,128)(2,1)}), bf16[64,8,512]{2,0,1:T(8,128)(2,1)S(1)}, u32[]{:S(2)}, u32[]{:S(2)}) %all-to-all-start.3) | async-done | bytes 524320 | tf_op jit(solution)/shard_map/all_to_all | solution.py:64
  49.1 1.5 convolution_convert_fusion
  51.3 5.3 %all-to-all-start.4 = ((bf16[64,8,128]{2,0,1:T(8,128)(2,1)}), bf16[64,8,128]{2,0,1:T(8,128)(2,1)}, u32[]{:S(2)}, u32[]{:S(2)}) async-start(bf16[64,8,128]{2,0,1:T(8,128)(2,1)} %copy_bitcast_fusion.4), calls=%async_computation.4 | async-start | bytes 262144 | tf_op jit(solution)/shard_map/all_to_all | solution.py:67
  58.6 4.8 %collective-permute-start.1 = (bf16[64,128]{0,1:T(8,128)(2,1)S(1)}, bf16[64,128]{0,1:T(8,128)(2,1)}, u32[]{:S(2)}, u32[]{:S(2)}) collective-permute-start(bf16[64,128]{0,1:T(8,128)(2,1)S(1)} %get-tuple-element.98), channel_id=1, source_target_pairs={{0,6},{1,7},{2,0},{3,1},{4,2},{5,3},{6,4},{7,5},{8,14},{9,15},{10,... | collective-permute-start | bytes 49160 | tf_op jit(solution)/shard_map/ppermute | solution.py:17
  63.4 1.9 collective-permute-start.2
  65.3 2.5 collective-permute-start.3
  67.8 3.6 %collective-permute-start.4 = (bf16[64,128]{0,1:T(8,128)(2,1)}, bf16[64,128]{0,1:T(8,128)(2,1)}, u32[]{:S(2)}, u32[]{:S(2)}) collective-permute-start(bf16[64,128]{0,1:T(8,128)(2,1)} %get-tuple-element.95), channel_id=1, source_target_pairs={{0,3},{1,4},{2,5},{3,6},{4,7},{5,0},{6,1},{7,2},{8,11},{9,12},{10,... | collective-permute-start | bytes 49160 | tf_op jit(solution)/shard_map/ppermute | solution.py:17
  72.3 6.0 %all-to-all-start.5 = ((bf16[64,8,512]{2,0,1:T(8,128)(2,1)}), bf16[64,8,512]{2,0,1:T(8,128)(2,1)S(1)}, u32[]{:S(2)}, u32[]{:S(2)}) async-start(bf16[64,8,512]{2,0,1:T(8,128)(2,1)} %bitcast.290), calls=%async_computation.5 | async-start | bytes 1048576 | tf_op jit(solution)/shard_map/all_to_all | solution.py:66
  78.3 3.4 %collective-permute-start.5 = (bf16[64,128]{0,1:T(8,128)(2,1)}, bf16[64,128]{0,1:T(8,128)(2,1)S(1)}, u32[]{:S(2)}, u32[]{:S(2)}) collective-permute-start(bf16[64,128]{0,1:T(8,128)(2,1)} %get-tuple-element.94), channel_id=1, source_target_pairs={{0,2},{1,3},{2,4},{3,5},{4,6},{5,7},{6,0},{7,1},{8,10},{9,11},{10,... | collective-permute-start | bytes 49160 | tf_op jit(solution)/shard_map/ppermute | solution.py:17
  81.7 1.7 compare_and_fusion
  84.7 1.9 copy.198
  86.6 70.3 %all-gather.1 = bf16[64,1,4]{2,1,0:T(2,128)(2,1)S(1)} all-gather(bf16[1,1,4]{2,1,0:T(2,128)(2,1)} %get-tuple-element.103), channel_id=1, replica_groups=mesh['ctx'=64,'uly'=8] {'ctx'}, dimensions={0}, use_global_device_ids=true | all-gather | bytes 520 | tf_op jit(solution)/shard_map/all_gather | solution.py:25
  157.9 1.1 concatenate.11
  159.8 1.3 collective-permute-start.8
  161.1 1.3 collective-permute-start.10
  162.4 1.3 collective-permute-start.9
  163.7 1.3 collective-permute-start.7
  165.0 4.5 %all-to-all-start.1 = ((bf16[64,8,512]{2,0,1:T(8,128)(2,1)}), bf16[64,8,512]{2,0,1:T(8,128)(2,1)S(1)}, u32[]{:S(2)}, u32[]{:S(2)}) async-start(bf16[64,8,512]{2,0,1:T(8,128)(2,1)} %bitcast.293), calls=%async_computation.1 | async-start | bytes 1048576 | tf_op jit(solution)/shard_map/all_to_all | solution.py:62
  169.7 1.8 fusion.6
  171.5 13.0 %collective-permute-done.9 = bf16[512,128]{1,0:T(8,128)(2,1)} collective-permute-done((bf16[512,128]{1,0:T(8,128)(2,1)}, bf16[512,128]{1,0:T(8,128)(2,1)}, u32[]{:S(2)}, u32[]{:S(2)}) %collective-permute-start.9) | collective-permute-done | bytes 131104 | tf_op jit(solution)/shard_map/ppermute | solution.py:45
  184.5 1.8 fusion
  186.3 1.8 fusion.3
  188.1 2.0 fusion.32
  192.9 2.0 fusion.29
  194.9 2.2 divide_convert_fusion
  198.6 4.4 %fusion.28 = f32[512,4,128]{0,2,1:T(8,128)} fusion(f32[4,512]{1,0:T(4,128)S(1)} %bitcast.311, pred[512,512]{1,0:T(8,128)(4,1)S(1)} %copy-done.5, bf16[512,4,128]{2,1,0:T(4,128)(2,1)} %copy-done.3, f32[512,4,128]{2,1,0:T(4,128)S(1)} %reshape.419, f32[512,4,128]{2,1,0:T(4,128)S(1)} %reshape.420), kind=kOutput, calls=%fused_computation.34 | convolution fusion | flops 545783808 | bytes 3940352 | tf_op jit(solution)/shard_map/hts,shd->thd/dot_general | solution.py:91
  203.1 10.8 %all-gather.4.cloned.1.call-done = bf16[256,128,128]{2,1,0:T(8,128)(2,1)} async-done(((bf16[4,128,128]{2,1,0:T(8,128)(2,1)}), bf16[256,128,128]{2,1,0:T(8,128)(2,1)}) %all-gather.4.cloned.1.call-update) | async-done | bytes 8388624 | tf_op jit(solution)/shard_map/all_gather | solution.py:25
  213.9 108.0 %while.12 = (s32[]{:T(128)}, f32[4,128,128]{2,1,0:T(8,128)S(1)}, s32[]{:T(128)}, bf16[64,4]{1,0:T(8,128)(2,1)}, bf16[64,4,128,128]{3,2,1,0:T(8,128)(2,1)}, /*index=5*/s32[]{:T(128)}, s32[]{:T(128)}, s32[]{:T(128)}) while((s32[]{:T(128)}, f32[4,128,128]{2,1,0:T(8,128)S(1)}, s32[]{:T(128)}, bf16[64,4]{1,0:T(8,128)(2,1)}, ...), condition=%wide.region_5.6_spmd, body=%wide.region_4.5_spmd.sunk | while | flops 196617 | bytes 655527 | solution.py:39
  214.6 1.0 convert_add_fusion.2
  216.3 1.0 convert_add_fusion.2
  218.0 1.0 convert_add_fusion.2
  219.8 1.0 convert_add_fusion.2
  221.5 1.0 convert_add_fusion.2
  223.2 1.0 convert_add_fusion.2
  224.9 1.0 convert_add_fusion.2
  228.4 1.0 convert_add_fusion.2
  230.1 1.0 convert_add_fusion.2
  231.8 1.0 convert_add_fusion.2
  233.5 1.0 convert_add_fusion.2
  321.9 1.8 multiply_reduce_fusion
  (213 shorter events, 113.6 us)
Async XLA Ops:
  7.2 43.5 %copy-start = (bf16[64,1024]{1,0:T(8,128)(2,1)S(1)}, bf16[64,1024]{1,0:T(8,128)(2,1)}, u32[]{:S(2)}) copy-start(bf16[64,1024]{1,0:T(8,128)(2,1)} %param.18) | copy-start | bytes 393220
  8.6 12.9 %all-to-all-start = ((bf16[8,2,128]{2,1,0:T(2,128)(2,1)}), bf16[8,2,128]{2,1,0:T(2,128)(2,1)S(1)}, u32[]{:S(2)}, u32[]{:S(2)}) async-start(bf16[8,2,128]{2,1,0:T(2,128)(2,1)} %reshape.433), calls=%async_computation | async-start | bytes 8192 | tf_op jit(solution)/shard_map/all_to_all | solution.py:65
  13.4 14.7 %copy-start.9 = (s32[512]{0:T(512)}, s32[512]{0:T(512)S(1)}, u32[]{:S(2)}) copy-start(s32[512]{0:T(512)S(1)} %get-tuple-element.124) | copy-start | bytes 6148
  13.4 14.7 %copy-start.7 = (s32[512]{0:T(512)}, s32[512]{0:T(512)S(1)}, u32[]{:S(2)}) copy-start(s32[512]{0:T(512)S(1)} %fusion.83) | copy-start | bytes 6148
  21.5 13.7 %all-to-all-start.2 = ((bf16[64,8,512]{2,0,1:T(8,128)(2,1)}), bf16[64,8,512]{2,0,1:T(8,128)(2,1)S(1)}, u32[]{:S(2)}, u32[]{:S(2)}) async-start(bf16[64,8,512]{2,0,1:T(8,128)(2,1)} %bitcast.292), calls=%async_computation.2 | async-start | bytes 1048576 | tf_op jit(solution)/shard_map/all_to_all | solution.py:63
  35.1 13.8 %all-to-all-start.3 = ((bf16[64,8,512]{2,0,1:T(8,128)(2,1)}), bf16[64,8,512]{2,0,1:T(8,128)(2,1)S(1)}, u32[]{:S(2)}, u32[]{:S(2)}) async-start(bf16[64,8,512]{2,0,1:T(8,128)(2,1)} %bitcast.291), calls=%async_computation.3 | async-start | bytes 1048576 | tf_op jit(solution)/shard_map/all_to_all | solution.py:64
  40.0 173.8 %all-gather.4.cloned.1.call-start = ((), (), s32[]{:S(2)}) async-start(), calls=%async_computation.6 | async-start | bytes 8519680 | tf_op jit(solution)/shard_map/all_gather | solution.py:25
  41.5 15.1 %copy-start.6 = (bf16[64,1024]{1,0:T(8,128)(2,1)S(1)}, bf16[64,1024]{1,0:T(8,128)(2,1)}, u32[]{:S(2)}) copy-start(bf16[64,1024]{1,0:T(8,128)(2,1)} %param.19) | copy-start | bytes 393220
  49.1 7.6 %copy-start.3 = (bf16[512,4,128]{2,1,0:T(4,128)(2,1)}, bf16[512,4,128]{2,1,0:T(4,128)(2,1)S(1)}, u32[]{:S(2)}) copy-start(bf16[512,4,128]{2,1,0:T(4,128)(2,1)S(1)} %reshape.408) | copy-start | bytes 1572868
  49.1 22.4 %copy-start.2 = (bf16[64,4096]{1,0:T(8,128)(2,1)S(1)}, bf16[64,4096]{1,0:T(8,128)(2,1)}, u32[]{:S(2)}) copy-start(bf16[64,4096]{1,0:T(8,128)(2,1)} %param.17) | copy-start | bytes 1572868
  49.1 32.6 %copy-start.8 = (s32[512]{0:T(512)S(1)}, s32[512]{0:T(512)}, u32[]{:S(2)}) copy-start(s32[512]{0:T(512)} %copy-done.7) | copy-start | bytes 6148
  49.1 32.6 %copy-start.10 = (s32[512]{0:T(512)S(1)}, s32[512]{0:T(512)}, u32[]{:S(2)}) copy-start(s32[512]{0:T(512)} %copy-done.9) | copy-start | bytes 6148
  49.1 32.6 %copy-start.11 = (s32[512]{0:T(512)S(1)}, s32[512]{0:T(512)}, u32[]{:S(2)}) copy-start(s32[512]{0:T(512)} %get-tuple-element.77) | copy-start | bytes 6148
  49.1 32.6 %copy-start.12 = (s32[512]{0:T(512)S(1)}, s32[512]{0:T(512)}, u32[]{:S(2)}) copy-start(s32[512]{0:T(512)} %get-tuple-element.79) | copy-start | bytes 6148
  50.6 107.2 %copy-start.1 = (f32[512,4]{1,0:T(8,128)S(1)}, f32[512,4]{1,0:T(8,128)}, u32[]{:S(2)}) copy-start(f32[512,4]{1,0:T(8,128)} %get-tuple-element.101) | copy-start | bytes 24580
  51.3 21.0 %all-to-all-start.4 = ((bf16[64,8,128]{2,0,1:T(8,128)(2,1)}), bf16[64,8,128]{2,0,1:T(8,128)(2,1)}, u32[]{:S(2)}, u32[]{:S(2)}) async-start(bf16[64,8,128]{2,0,1:T(8,128)(2,1)} %copy_bitcast_fusion.4), calls=%async_computation.4 | async-start | bytes 262144 | tf_op jit(solution)/shard_map/all_to_all | solution.py:67
  58.4 19.8 %collective-permute-start = (bf16[64,128]{0,1:T(8,128)(2,1)S(1)}, bf16[64,128]{0,1:T(8,128)(2,1)}, u32[]{:S(2)}, u32[]{:S(2)}) collective-permute-start(bf16[64,128]{0,1:T(8,128)(2,1)S(1)} %get-tuple-element.99), channel_id=1, source_target_pairs={{0,7},{1,0},{2,1},{3,2},{4,3},{5,4},{6,5},{7,6},{8,15},{9,8},{10,9... | collective-permute-start | bytes 49160 | tf_op jit(solution)/shard_map/ppermute | solution.py:17
  58.6 23.1 %collective-permute-start.1 = (bf16[64,128]{0,1:T(8,128)(2,1)S(1)}, bf16[64,128]{0,1:T(8,128)(2,1)}, u32[]{:S(2)}, u32[]{:S(2)}) collective-permute-start(bf16[64,128]{0,1:T(8,128)(2,1)S(1)} %get-tuple-element.98), channel_id=1, source_target_pairs={{0,6},{1,7},{2,0},{3,1},{4,2},{5,3},{6,4},{7,5},{8,14},{9,15},{10,... | collective-permute-start | bytes 49160 | tf_op jit(solution)/shard_map/ppermute | solution.py:17
  63.4 94.5 %collective-permute-start.2 = (bf16[64,128]{0,1:T(8,128)(2,1)}, bf16[64,128]{0,1:T(8,128)(2,1)}, u32[]{:S(2)}, u32[]{:S(2)}) collective-permute-start(bf16[64,128]{0,1:T(8,128)(2,1)} %get-tuple-element.97), channel_id=1, source_target_pairs={{0,5},{1,6},{2,7},{3,0},{4,1},{5,2},{6,3},{7,4},{8,13},{9,14},{10,... | collective-permute-start | bytes 49160 | tf_op jit(solution)/shard_map/ppermute | solution.py:17
  65.3 92.6 %collective-permute-start.3 = (bf16[64,128]{0,1:T(8,128)(2,1)}, bf16[64,128]{0,1:T(8,128)(2,1)}, u32[]{:S(2)}, u32[]{:S(2)}) collective-permute-start(bf16[64,128]{0,1:T(8,128)(2,1)} %get-tuple-element.96), channel_id=1, source_target_pairs={{0,4},{1,5},{2,6},{3,7},{4,0},{5,1},{6,2},{7,3},{8,12},{9,13},{10,... | collective-permute-start | bytes 49160 | tf_op jit(solution)/shard_map/ppermute | solution.py:17
  67.8 90.0 %collective-permute-start.4 = (bf16[64,128]{0,1:T(8,128)(2,1)}, bf16[64,128]{0,1:T(8,128)(2,1)}, u32[]{:S(2)}, u32[]{:S(2)}) collective-permute-start(bf16[64,128]{0,1:T(8,128)(2,1)} %get-tuple-element.95), channel_id=1, source_target_pairs={{0,3},{1,4},{2,5},{3,6},{4,7},{5,0},{6,1},{7,2},{8,11},{9,12},{10,... | collective-permute-start | bytes 49160 | tf_op jit(solution)/shard_map/ppermute | solution.py:17
  72.3 85.6 %copy-start.4 = (bf16[64,128]{0,1:T(8,128)(2,1)S(1)}, bf16[64,128]{0,1:T(8,128)(2,1)}, u32[]{:S(2)}) copy-start(bf16[64,128]{0,1:T(8,128)(2,1)} %get-tuple-element.92) | copy-start | bytes 49156
  72.3 92.7 %all-to-all-start.5 = ((bf16[64,8,512]{2,0,1:T(8,128)(2,1)}), bf16[64,8,512]{2,0,1:T(8,128)(2,1)S(1)}, u32[]{:S(2)}, u32[]{:S(2)}) async-start(bf16[64,8,512]{2,0,1:T(8,128)(2,1)} %bitcast.290), calls=%async_computation.5 | async-start | bytes 1048576 | tf_op jit(solution)/shard_map/all_to_all | solution.py:66
  78.3 79.6 %collective-permute-start.5 = (bf16[64,128]{0,1:T(8,128)(2,1)}, bf16[64,128]{0,1:T(8,128)(2,1)S(1)}, u32[]{:S(2)}, u32[]{:S(2)}) collective-permute-start(bf16[64,128]{0,1:T(8,128)(2,1)} %get-tuple-element.94), channel_id=1, source_target_pairs={{0,2},{1,3},{2,4},{3,5},{4,6},{5,7},{6,0},{7,1},{8,10},{9,11},{10,... | collective-permute-start | bytes 49160 | tf_op jit(solution)/shard_map/ppermute | solution.py:17
  81.7 76.2 %collective-permute-start.6 = (bf16[64,128]{0,1:T(8,128)(2,1)}, bf16[64,128]{0,1:T(8,128)(2,1)S(1)}, u32[]{:S(2)}, u32[]{:S(2)}) collective-permute-start(bf16[64,128]{0,1:T(8,128)(2,1)} %get-tuple-element.93), channel_id=1, source_target_pairs={{0,1},{1,2},{2,3},{3,4},{4,5},{5,6},{6,7},{7,0},{8,9},{9,10},{10,1... | collective-permute-start | bytes 49160 | tf_op jit(solution)/shard_map/ppermute | solution.py:17
  159.8 28.3 %collective-permute-start.8 = (bf16[512,128]{0,1:T(8,128)(2,1)}, bf16[512,128]{0,1:T(8,128)(2,1)}, u32[]{:S(2)}, u32[]{:S(2)}) collective-permute-start(bf16[512,128]{0,1:T(8,128)(2,1)} %constant_dynamic-slice_fusion), channel_id=1, source_target_pairs={{0,8},{8,16},{16,24},{24,32},{32,40},{40,48},{48,56},{56,64},{64,7... | collective-permute-start | bytes 393224 | tf_op jit(solution)/shard_map/ppermute | solution.py:45
  161.1 31.8 %collective-permute-start.10 = (bf16[512,128]{0,1:T(8,128)(2,1)}, bf16[512,128]{0,1:T(8,128)(2,1)}, u32[]{:S(2)}, u32[]{:S(2)}) collective-permute-start(bf16[512,128]{0,1:T(8,128)(2,1)} %constant_dynamic-slice_fusion), channel_id=1, source_target_pairs={{0,16},{8,24},{16,32},{24,40},{32,48},{40,56},{48,64},{56,72},{64,... | collective-permute-start | bytes 393224 | tf_op jit(solution)/shard_map/ppermute | solution.py:45
  162.4 22.1 %collective-permute-start.9 = (bf16[512,128]{1,0:T(8,128)(2,1)}, bf16[512,128]{1,0:T(8,128)(2,1)}, u32[]{:S(2)}, u32[]{:S(2)}) collective-permute-start(bf16[512,128]{1,0:T(8,128)(2,1)} %bitcast.20), channel_id=1, source_target_pairs={{0,16},{8,24},{16,32},{24,40},{32,48},{40,56},{48,64},{56,72},{64,... | collective-permute-start | bytes 393224 | tf_op jit(solution)/shard_map/ppermute | solution.py:45
  163.7 22.6 %collective-permute-start.7 = (bf16[512,128]{1,0:T(8,128)(2,1)}, bf16[512,128]{1,0:T(8,128)(2,1)}, u32[]{:S(2)}, u32[]{:S(2)}) collective-permute-start(bf16[512,128]{1,0:T(8,128)(2,1)} %bitcast.20), channel_id=1, source_target_pairs={{0,8},{8,16},{16,24},{24,32},{32,40},{40,48},{48,56},{56,64},{64,7... | collective-permute-start | bytes 393224 | tf_op jit(solution)/shard_map/ppermute | solution.py:45
  165.0 33.1 %all-to-all-start.1 = ((bf16[64,8,512]{2,0,1:T(8,128)(2,1)}), bf16[64,8,512]{2,0,1:T(8,128)(2,1)S(1)}, u32[]{:S(2)}, u32[]{:S(2)}) async-start(bf16[64,8,512]{2,0,1:T(8,128)(2,1)} %bitcast.293), calls=%async_computation.1 | async-start | bytes 1048576 | tf_op jit(solution)/shard_map/all_to_all | solution.py:62
  197.1 1.5 copy-start.5
  213.9 109.8 %copy-start.13 = (f32[512]{0:T(512)S(1)}, f32[512]{0:T(512)}, u32[]{:S(2)}) copy-start(f32[512]{0:T(512)} %param.15) | copy-start | bytes 6148
Sparse Core Ops, SparseCore 0:
  50.7 163.0 all-gather.3
